TPU v7x, 32 devices: a whole 2x2x4 slice. The times are simulated.
32 devices in a mesh: ex: 16 (over z, x, core), feat: 2 (over y).
Axes of the slice: x: 2, y: 2, z: 4, core: 2. Of those that a mesh axis runs over, the one named last changes fastest.
Arguments:
- features: bfloat16 [1536, 8192], P('ex', 'feat'), may hold values from -100 to 100
Outputs:
- kernel: float32 [1536, 1536], P('ex', 'feat')
All inputs are finite; a program needn't handle non-finite values.
Results may differ from a plain program's by a relative error of at most 0.0003.
Values may be sent and summed in bfloat16 or wider, within the bound.
A program may use at most 64 MiB of HBM per device.

v0:
```python
import jax
import jax.numpy as jnp
from jax import lax
from jax.sharding import PartitionSpec as P


def inner_tile(left, right):
    return lax.dot_general(
        left, right, (((1,), (1,)), ((), ())), preferred_element_type=jnp.float32
    )


def shards(features):
    local_squares = jnp.sum(jnp.square(features.astype(jnp.float32)), axis=1)
    row_norms = lax.psum(local_squares, "feat")
    every_norm = lax.all_gather(row_norms, "ex", axis=0, tiled=True)
    partial_gram = inner_tile(features, lax.all_gather(features, "ex", axis=0, tiled=True))
    gram = lax.psum_scatter(partial_gram, "feat", scatter_dimension=1, tiled=True)
    col_width = gram.shape[1]
    col_norms = lax.dynamic_slice_in_dim(
        every_norm, lax.axis_index("feat") * col_width, col_width, 0
    )
    row_scale = lax.rsqrt(row_norms + 1e-06)
    col_scale = lax.rsqrt(col_norms + 1e-06)
    return gram * row_scale[:, None] * col_scale[None, :]


def solution(mesh):
    placed = (P("ex", "feat"),)
    return jax.shard_map(
        shards, mesh=mesh, in_specs=placed, out_specs=P("ex", "feat"), check_vma=False
    )
```

profile of v0, /device:TPU:0, one launch (start us, length us, event | category | flops | bytes accessed | tf_op | source)
XLA Modules:
  0.0 168.3 jit_solution(15875303904198936587)
XLA Ops:
  6.5 0.0 copy-start.1
  6.5 0.0 copy-start
  6.5 0.0 all-gather.2.cloned.1.call-start
  6.5 0.7 all-gather.2.cloned.1.call-update
  7.3 0.0 reduce-scatter.2.cloned.1.call-start
  7.3 105.8 %all-gather.2.cloned.1.call-done = bf16[1536,4096]{1,0:T(8,128)(2,1)} async-done(((bf16[96,4096]{1,0:T(8,128)(2,1)}), bf16[1536,4096]{1,0:T(8,128)(2,1)}) %all-gather.2.cloned.1.call-update) | async-done | bytes 12582928 | tf_op jit(solution)/shard_map/all_gather | solution.py:17
  113.1 9.7 %fusion = f32[96,1536]{1,0:T(8,128)} fusion(bf16[96,4096]{1,0:T(8,128)(2,1)} %param.1, bf16[1536,4096]{1,0:T(8,128)(2,1)} %all-gather.2.cloned.1.call-done), kind=kOutput, calls=%fused_computation.4 | convolution fusion | flops 1207959552 | bytes 13959168 | tf_op jit(solution)/shard_map/dot_general | solution.py:8
  122.8 0.0 reduce-scatter.2.cloned.1.call-update
  122.8 0.0 copy-done.1
  122.8 0.6 dynamic-slice
  124.1 0.0 copy-done
  124.1 0.3 multiply_reduce_fusion
  124.3 4.9 %psum.7 = f32[96]{0:T(128)S(1)} all-reduce(f32[96]{0:T(128)S(1)} %multiply_reduce_fusion), channel_id=1, replica_groups=mesh['ex'=16,'feat'=2] {'feat'}, use_global_device_ids=true, to_apply=%region_2.0 | all-reduce | flops 96 | bytes 768 | tf_op jit(solution)/shard_map/psum | solution.py:15
  129.3 0.2 dynamic-update-slice
  129.5 30.1 %all-reduce = f32[1536]{0:T(1024)S(1)} all-reduce(f32[1536]{0:T(1024)S(1)} %dynamic-update-slice), channel_id=1, replica_groups=mesh['ex'=16,'feat'=2] {'ex'}, use_global_device_ids=true, to_apply=%add | all-reduce | flops 1536 | bytes 12288
  159.6 0.1 add_rsqrt_fusion
  159.7 0.0 reduce-scatter.2.cloned.1.call-done
  159.7 1.8 %multiply_multiply_fusion = f32[96,768]{1,0:T(8,128)} fusion(f32[96,768]{1,0:T(8,128)} %reduce-scatter.2.cloned.1.call-done, f32[768]{0:T(1024)S(1)} %add_rsqrt_fusion, f32[96]{0:T(128)S(1)} %add_rsqrt_fusion.1), kind=kLoop, calls=%fused_computation.1 | loop fusion | flops 147456 | bytes 593280 | tf_op jit(solution)/shard_map/mul | solution.py:25
  (2 shorter events, 0.0 us)
Async XLA Ops:
  6.5 116.3 %copy-start.1 = (u32[32]{0:T(128)S(1)}, u32[32]{0:T(128)}, u32[]{:S(2)}) copy-start(u32[32]{0:T(128)} %constant.17) | copy-start | bytes 388
  6.5 117.5 %copy-start = (bf16[96,4096]{1,0:T(8,128)(2,1)S(1)}, bf16[96,4096]{1,0:T(8,128)(2,1)}, u32[]{:S(2)}) copy-start(bf16[96,4096]{1,0:T(8,128)(2,1)} %param.1) | copy-start | bytes 2359300
  6.5 106.6 %all-gather.2.cloned.1.call-start = ((), (), s32[]{:S(2)}) async-start(), calls=%async_computation.1 | async-start | bytes 13369344 | tf_op jit(solution)/shard_map/all_gather | solution.py:17
  7.3 152.4 %reduce-scatter.2.cloned.1.call-start = ((), (), s32[]{:S(2)}) async-start(), calls=%async_computation.2 | async-start | bytes 884736 | tf_op jit(solution)/shard_map/reduce_scatter | solution.py:18
Sparse Core Ops, SparseCore 0:
  9.6 103.4 all-gather.1
  123.0 13.4 reduce-scatter.1
where the time goes:
time: 169 us; the launch traced here: 168 us
  waiting for transfers between devices  107 us (63%)
  blocking collectives  35.1 us (21%)
  between operations  14.1 us (8%)
  matrix products  9.67 us (6%)
  other arithmetic  2.12 us (1%)
    all_gather x1, waiting for transfers between devices, shards(): lax.all_gather(features, 'ex', axis=0, tiled=True)  106 us
    unnamed x1, blocking collectives  30.1 us
    dot_general x1, matrix products, inner_tile(): lax.dot_general(left, right, (((1,), (1,)), ((), ())), preferred_element_...  9.67 us
    psum x1, blocking collectives, shards(): row_norms = lax.psum(local_squares, 'feat')  4.94 us
  transfers between devices with their start and end apart: 2, of which 1 were waited for; matrix products, arithmetic and copies ran while one was open for 1% of the time, Pallas kernels for 0%

commit v1 on v0

v1 whole, which is shorter than its diff:
```python
import jax
import jax.numpy as jnp
from jax import lax
from jax.experimental import pallas as pl
from jax.experimental.pallas import tpu as pltpu
from jax.sharding import PartitionSpec as P

MESH = pl.DeviceIdType.MESH
EPS = 1e-06
DEPTH_STEP = 1024
STAT_ROWS = 8


def inner_tile(left, right):
    return lax.dot_general(
        left, right, (((1,), (1,)), ((), ())), preferred_element_type=jnp.float32
    )


def lane_squares(block):
    depth = block.shape[-1]
    total = None
    for start in range(0, depth, 128):
        value = block[:, start : start + 128].astype(jnp.float32)
        total = value * value if total is None else total + value * value
    return total


def hub_kernel(
    f_ref, o_ref, near, far, rows, tiles, landed, squares, send, recv, tile_send, tile_recv, local
):
    n, depth = f_ref.shape
    e, y = lax.axis_index("ex"), lax.axis_index("feat")
    z, x, c = e // 4, (e // 2) % 2, e % 2
    h = z // 2
    ox, oc, oy, oh = 1 - x, 1 - c, 1 - y, 1 - h
    hub_z, end_z = 1 + h, 3 * h
    far_hub_z, far_end_z = 1 + oh, 3 * oh
    is_hub = z == hub_z

    def at(z_, x_, c_):
        return z_ * 4 + x_ * 2 + c_

    def remote(src, dst, number, to, to_y):
        return pltpu.make_async_remote_copy(
            src_ref=src,
            dst_ref=dst,
            send_sem=send.at[number],
            recv_sem=recv.at[number],
            device_id=(to, to_y),
            device_id_type=MESH,
        )

    barrier = pltpu.get_barrier_semaphore()

    def greet(i, carry):
        to, to_y = 8 * h + i // 2, i % 2

        @pl.when(jnp.logical_or(to != e, to_y != y))
        def _():
            pl.semaphore_signal(barrier, inc=1, device_id=(to, to_y), device_id_type=MESH)

        return carry

    lax.fori_loop(0, 16, greet, 0)
    pl.semaphore_signal(
        barrier, inc=1, device_id=(at(far_hub_z, x, c), y), device_id_type=MESH
    )

    @pl.when(is_hub)
    def _():
        pl.semaphore_signal(
            barrier, inc=1, device_id=(at(far_end_z, x, c), y), device_id_type=MESH
        )
        pl.semaphore_wait(barrier, 17)

    @pl.when(jnp.logical_not(is_hub))
    def _():
        pl.semaphore_wait(barrier, 16)

    near_end = remote(f_ref, near.at[h], 0, at(hub_z, x, c), y)
    far_end = remote(f_ref, far.at[h], 2, at(far_hub_z, x, c), y)
    far_hub = remote(f_ref, far.at[oh], 1, at(far_hub_z, x, c), y)
    swap_squares = remote(squares.at[0], squares.at[1], 9, e, oy)

    def send_squares():
        own = jnp.sum(lane_squares(f_ref[...]), axis=1, keepdims=True)
        squares[0] = jnp.broadcast_to(own, (n, 128))
        swap_squares.start()

    @pl.when(jnp.logical_not(is_hub))
    def _():
        near_end.start()
        send_squares()
        near_end.wait_send()
        far_end.start()
        far_end.wait_send()

    def multiply(kind, columns, first, last):
        count = last - first
        for step in range(depth // DEPTH_STEP):
            piece = pl.ds(step * DEPTH_STEP, DEPTH_STEP)
            left = rows[first:last, :, piece].reshape(count * n, DEPTH_STEP)
            right = columns[:, :, piece].reshape(2 * n, DEPTH_STEP)
            product = inner_tile(left, right).reshape(count, n, 2 * n)
            if step == 0:
                tiles[kind, first:last, 0:n, :] = product
            else:
                tiles[kind, first:last, 0:n, :] += product

    def column_squares(kind, columns):
        lanes = lane_squares(columns[...].reshape(2 * n, depth))
        total = jnp.sum(jnp.transpose(lanes), axis=0, keepdims=True)
        tiles[kind, :, n : n + STAT_ROWS, :] = jnp.broadcast_to(
            total[None], (8, STAT_ROWS, 2 * n)
        )

    def tile_copy(kind, r, to, to_y):
        return pltpu.make_async_remote_copy(
            src_ref=tiles.at[kind, r],
            dst_ref=landed.at[y, x, c],
            send_sem=tile_send.at[kind, r],
            recv_sem=tile_recv.at[y, x, c],
            device_id=(to, to_y),
            device_id_type=MESH,
        )

    def own_tile(kind, r):
        return pltpu.make_async_copy(
            tiles.at[kind, r], landed.at[y, x, c], tile_recv.at[y, x, c]
        )

    def deliver(kind, first, last):
        to_y = h if kind == 0 else oh

        def one(r, carry):
            to_z = jnp.where((r // 2) % 2 == 0, hub_z, end_z)
            to = at(to_z, jnp.where(r // 4 == 0, x, ox), r % 2)
            mine = jnp.logical_and(to == e, to_y == y)

            @pl.when(mine)
            def _():
                own_tile(kind, r).start()

            @pl.when(jnp.logical_not(mine))
            def _():
                tile_copy(kind, r, to, to_y).start()

            return carry

        lax.fori_loop(first, last, one, 0)

    def drain(kind):
        to_y = h if kind == 0 else oh

        def one(r, carry):
            mine = jnp.logical_and(r == c, to_y == y)

            @pl.when(jnp.logical_not(mine))
            def _():
                tile_copy(kind, r, e, oy).wait_send()

            return carry

        lax.fori_loop(0, 8, one, 0)

    @pl.when(is_hub)
    def _():
        to_x = at(hub_z, ox, c)
        to_core = at(hub_z, x, oc)
        hub_to_x = remote(f_ref, rows.at[4 + c], 3, to_x, y)
        hub_to_core = remote(f_ref, rows.at[c], 5, to_core, y)
        end_to_x = remote(near.at[h], rows.at[6 + c], 4, to_x, y)
        end_to_core = remote(near.at[h], rows.at[2 + c], 6, to_core, y)
        other_hub_to_core = remote(rows.at[4 + c], rows.at[4 + c], 7, to_core, y)
        other_end_to_core = remote(rows.at[6 + c], rows.at[6 + c], 8, to_core, y)
        from_core = [
            remote(rows.at[2 * i + oc], rows.at[2 * i + oc], 5 + i, to_core, y)
            for i in range(4)
        ]
        far_hub.start()
        hub_to_x.start()
        hub_to_core.start()
        keep = [
            pltpu.make_async_copy(f_ref, near.at[oh], local.at[0]),
            pltpu.make_async_copy(f_ref, rows.at[c], local.at[1]),
            pltpu.make_async_copy(near.at[h], rows.at[2 + c], local.at[2]),
        ]
        keep[0].start()
        keep[1].start()
        send_squares()
        near_end.wait_recv()
        end_to_x.start()
        end_to_core.start()
        keep[2].start()
        hub_to_x.wait_recv()
        other_hub_to_core.start()
        for copy in keep:
            copy.wait()
        column_squares(0, near)
        from_core[0].wait_recv()
        from_core[1].wait_recv()
        from_core[2].wait_recv()
        multiply(0, near, 0, 6)
        deliver(0, 0, 6)
        end_to_x.wait_recv()
        other_end_to_core.start()
        far_hub.wait_recv()
        far_end.wait_recv()
        from_core[3].wait_recv()
        column_squares(1, far)
        multiply(1, far, 0, 8)
        deliver(1, 0, 8)
        multiply(0, near, 6, 8)
        deliver(0, 6, 8)
        for copy in (
            far_hub, hub_to_x, hub_to_core, end_to_x, end_to_core,
            other_hub_to_core, other_end_to_core,
        ):
            copy.wait_send()

    swap_squares.wait()
    row_scale = lax.rsqrt(squares[0][:, 0:1] + squares[1][:, 0:1] + EPS)
    for x_ in range(2):
        for c_ in range(2):
            for y_ in range(2):
                pltpu.make_async_copy(
                    landed.at[y_, x_, c_], landed.at[y_, x_, c_], tile_recv.at[y_, x_, c_]
                ).wait()
            total = landed[0, x_, c_] + landed[1, x_, c_]
            column_scale = lax.rsqrt(total[n : n + 1] + EPS)
            o_ref[2 * x_ + c_] = total[0:n] * row_scale * column_scale

    @pl.when(is_hub)
    def _():
        drain(0)
        drain(1)


def hub_shards(features):
    n, depth = features.shape
    pieces = pl.pallas_call(
        hub_kernel,
        out_shape=jax.ShapeDtypeStruct((4, n, 2 * n), jnp.float32),
        in_specs=[pl.BlockSpec(memory_space=pltpu.VMEM)],
        out_specs=pl.BlockSpec(memory_space=pltpu.VMEM),
        scratch_shapes=[
            pltpu.VMEM((2, n, depth), jnp.bfloat16),
            pltpu.VMEM((2, n, depth), jnp.bfloat16),
            pltpu.VMEM((8, n, depth), jnp.bfloat16),
            pltpu.VMEM((2, 8, n + STAT_ROWS, 2 * n), jnp.float32),
            pltpu.VMEM((2, 2, 2, n + STAT_ROWS, 2 * n), jnp.float32),
            pltpu.VMEM((2, n, 128), jnp.float32),
            pltpu.SemaphoreType.DMA((10,)),
            pltpu.SemaphoreType.DMA((10,)),
            pltpu.SemaphoreType.DMA((2, 8)),
            pltpu.SemaphoreType.DMA((2, 2, 2)),
            pltpu.SemaphoreType.DMA((3,)),
        ],
        compiler_params=pltpu.CompilerParams(
            collective_id=0, has_side_effects=True, vmem_limit_bytes=40 * 1024 * 1024
        ),
        name="hub_gram",
    )(features)
    pieces = pieces.reshape(2, 2, n, 2, n)
    return jnp.transpose(pieces, (2, 3, 0, 1, 4)).reshape(n, 8 * n)


def gathered_shards(features):
    local_squares = jnp.sum(jnp.square(features.astype(jnp.float32)), axis=1)
    row_norms = lax.psum(local_squares, "feat")
    every_norm = lax.all_gather(row_norms, "ex", axis=0, tiled=True)
    partial_gram = inner_tile(features, lax.all_gather(features, "ex", axis=0, tiled=True))
    gram = lax.psum_scatter(partial_gram, "feat", scatter_dimension=1, tiled=True)
    col_width = gram.shape[1]
    col_norms = lax.dynamic_slice_in_dim(
        every_norm, lax.axis_index("feat") * col_width, col_width, 0
    )
    row_scale = lax.rsqrt(row_norms + EPS)
    col_scale = lax.rsqrt(col_norms + EPS)
    return gram * row_scale[:, None] * col_scale[None, :]


def solution(mesh):
    four_groups = mesh.shape["ex"] == 16 and mesh.shape["feat"] == 2
    shards = hub_shards if four_groups else gathered_shards
    return jax.shard_map(
        shards,
        mesh=mesh,
        in_specs=(P("ex", "feat"),),
        out_specs=P("ex", "feat"),
        check_vma=False,
    )
```

time: 169 us -> 65.2 us (0.39)
  waiting for transfers between devices: 107 us -> 0 us
  Pallas kernels: 0 us -> 61.6 us
  blocking collectives: 35.1 us -> 0 us
  between operations: 14.1 us -> 0.03 us
  matrix products: 9.67 us -> 0 us
  other arithmetic: 2.12 us -> 0 us
  local copies, waits for them, and re-layouts: 0.78 us -> 2.88 us
    all_gather x1 -> x0, waiting for transfers between devices: 106 us -> none  [shards(): lax.all_gather(features, 'ex', axis=0, tiled=True)]
    pallas_call x0 -> x1, Pallas kernels: none -> 61.6 us  [hub_shards(): pl.pallas_call(hub_kernel, out_shape=jax.ShapeDtypeStruct((4, n, 2 * n),...]
    unnamed x1 -> x0, blocking collectives: 30.1 us -> none
    dot_general x1 -> x0, matrix products: 9.67 us -> none  [inner_tile(): lax.dot_general(left, right, (((1,), (1,)), ((), ())), preferred_element_...]
    psum x1 -> x0, blocking collectives: 4.94 us -> none  [shards(): row_norms = lax.psum(local_squares, 'feat')]
    mul x1 -> x0, other arithmetic: 1.78 us -> none  [shards(): return gram * row_scale[:, None] * col_scale[None, :]]
  transfers between devices with their start and end apart: 2 -> 0, of which waited for: 1 -> 0; matrix products, arithmetic and copies ran while one was open for 1% -> 0% of each run, Pallas kernels for 0% -> 0%
where the time goes in v1:
time: 65.2 us; the launch traced here: 64.5 us
  Pallas kernels  61.6 us (94%)
  local copies, waits for them, and re-layouts  2.88 us (4%)
    pallas_call x1, Pallas kernels, hub_shards(): pl.pallas_call(hub_kernel, out_shape=jax.ShapeDtypeStruct((4, n, 2 * n),...  61.6 us

profile of v1, /device:TPU:0, one launch (start us, length us, event | category | flops | bytes accessed | tf_op | source)
XLA Modules:
  0.0 64.5 jit_solution(5630840135599908801)
XLA Ops:
  0.0 0.0 copy-start
  0.0 1.1 %copy-done = bf16[96,4096]{1,0:T(8,128)(2,1)S(1)} copy-done((bf16[96,4096]{1,0:T(8,128)(2,1)S(1)}, bf16[96,4096]{1,0:T(8,128)(2,1)}, u32[]{:S(2)}) %copy-start) | copy-done | bytes 786456
  1.1 61.6 %hub_gram.1 = f32[4,96,192]{2,1,0:T(8,128)S(1)} custom-call(bf16[96,4096]{1,0:T(8,128)(2,1)S(1)} %copy-done), custom_call_target="tpu_custom_call" | custom-call | tf_op jit(solution)/shard_map/hub_gram/pallas_call | solution.py:242
  62.7 0.3 reshape.6
  63.0 0.3 copy.2
  63.3 1.2 %reshape.7 = f32[96,768]{1,0:T(8,128)} reshape(f32[96,2,2,2,96]{4,3,2,1,0:T(2,128)S(1)} %copy.2) | data formatting | bytes 589824 | tf_op jit(solution)/shard_map/reshape | solution.py:266
Async XLA Ops:
  0.0 1.1 %copy-start = (bf16[96,4096]{1,0:T(8,128)(2,1)S(1)}, bf16[96,4096]{1,0:T(8,128)(2,1)}, u32[]{:S(2)}) copy-start(bf16[96,4096]{1,0:T(8,128)(2,1)} %f_ref.1) | copy-start | bytes 2359300

commit v2 on v1

v2 whole, which is shorter than its diff:
```python
import jax
import jax.numpy as jnp
from jax import lax
from jax.experimental import pallas as pl
from jax.experimental.pallas import tpu as pltpu
from jax.sharding import PartitionSpec as P

MESH = pl.DeviceIdType.MESH
EPS = 1e-06
DEPTH_STEP = 1024
STAT_ROWS = 8
PIECES = 4


def inner_tile(left, right):
    return lax.dot_general(
        left, right, (((1,), (1,)), ((), ())), preferred_element_type=jnp.float32
    )


def lane_squares(block):
    depth = block.shape[-1]
    total = None
    for start in range(0, depth, 128):
        value = block[:, start : start + 128].astype(jnp.float32)
        total = value * value if total is None else total + value * value
    return total


def fold(block, pad):
    n = block.shape[0]
    kept = n - pad
    free = 128 - n
    tail = block[kept:n]
    extra = [tail[:, i * free : (i + 1) * free] for i in range(n // free)]
    return jnp.concatenate([block[0:kept], jnp.concatenate(extra, axis=0)], axis=1)


def unfold(folded, pad):
    n = folded.shape[0] + pad
    free = 128 - n
    extra = folded[:, n:128]
    tail = [extra[i * pad : (i + 1) * pad] for i in range(n // free)]
    return jnp.concatenate([folded[:, 0:n], jnp.concatenate(tail, axis=1)], axis=0)


def hub_kernel(
    f_ref, o_ref, cols, rows, acc, tiles, landed, squares, send, recv, tile_send, tile_recv, local
):
    n, depth = f_ref.shape
    pad = n * (128 - n) // 128
    kept = n - pad
    e, y = lax.axis_index("ex"), lax.axis_index("feat")
    z, x, c = e // 4, (e // 2) % 2, e % 2
    h = z // 2
    ox, oc, oy, oh = 1 - x, 1 - c, 1 - y, 1 - h
    hub_z, end_z = 1 + h, 3 * h
    far_hub_z, far_end_z = 1 + oh, 3 * oh
    is_hub = z == hub_z
    width = depth // PIECES

    def at(z_, x_, c_):
        return z_ * 4 + x_ * 2 + c_

    def remote(src, dst, number, to, to_y):
        return pltpu.make_async_remote_copy(
            src_ref=src,
            dst_ref=dst,
            send_sem=send.at[number],
            recv_sem=recv.at[number],
            device_id=(to, to_y),
            device_id_type=MESH,
        )

    def remote_pieces(src, dst, number, to, to_y):
        return [
            remote(
                src.at[:, pl.ds(k * width, width)],
                dst.at[:, pl.ds(k * width, width)],
                number + k,
                to,
                to_y,
            )
            for k in range(PIECES)
        ]

    own = pltpu.make_async_copy(f_ref, cols.at[1], local.at[0])
    own.start()

    barrier = pltpu.get_barrier_semaphore()

    def greet(i, carry):
        to, to_y = 8 * h + i // 2, i % 2

        @pl.when(jnp.logical_or(to != e, to_y != y))
        def _():
            pl.semaphore_signal(barrier, inc=1, device_id=(to, to_y), device_id_type=MESH)

        return carry

    lax.fori_loop(0, 16, greet, 0)
    pl.semaphore_signal(
        barrier, inc=1, device_id=(at(far_hub_z, x, c), y), device_id_type=MESH
    )

    @pl.when(is_hub)
    def _():
        pl.semaphore_signal(
            barrier, inc=1, device_id=(at(far_end_z, x, c), y), device_id_type=MESH
        )
        pl.semaphore_wait(barrier, 17)

    @pl.when(jnp.logical_not(is_hub))
    def _():
        pl.semaphore_wait(barrier, 16)

    near_end = remote(f_ref, cols.at[0], 0, at(hub_z, x, c), y)
    far_hub = remote(f_ref, cols.at[2], 1, at(far_hub_z, x, c), y)
    far_end = remote_pieces(f_ref, cols.at[3], 8, at(far_hub_z, x, c), y)
    swap_squares = remote(squares.at[0], squares.at[1], 2, e, oy)

    def send_squares():
        own.wait()
        total = jnp.sum(lane_squares(cols[1]), axis=1, keepdims=True)
        squares[0] = jnp.broadcast_to(total, (n, 128))
        swap_squares.start()

    @pl.when(jnp.logical_not(is_hub))
    def _():
        near_end.start()
        send_squares()
        near_end.wait_send()
        for copy in far_end:
            copy.start()
        for copy in far_end:
            copy.wait_send()

    def multiply(j, first, last, start, size, fresh):
        count = last - first
        for step in range(size // DEPTH_STEP):
            piece = pl.ds(start + step * DEPTH_STEP, DEPTH_STEP)
            left = rows[first:last, :, piece].reshape(count * n, DEPTH_STEP)
            product = inner_tile(left, cols[j, :, piece]).reshape(count, n, n)
            if fresh and step == 0:
                acc[j, first:last] = product
            else:
                acc[j, first:last] += product

    def column_squares(j):
        lanes = lane_squares(cols[j])
        total = jnp.sum(jnp.transpose(lanes), axis=0, keepdims=True)
        tiles[j, :, kept : kept + STAT_ROWS, 0:n] = jnp.broadcast_to(
            total[None], (8, STAT_ROWS, n)
        )

    def tile_copy(j, r, to, to_y, group):
        return pltpu.make_async_remote_copy(
            src_ref=tiles.at[j, r],
            dst_ref=landed.at[y, x, c, group],
            send_sem=tile_send.at[j, r],
            recv_sem=tile_recv.at[y, x, c, group],
            device_id=(to, to_y),
            device_id_type=MESH,
        )

    def place(j):
        to_y = h if j < 2 else oh
        group = h if j in (0, 2) else oh
        return to_y, group

    def deliver(j, first, last):
        to_y, group = place(j)

        def one(r, carry):
            tiles[j, r, 0:kept, :] = fold(acc[j, r], pad)
            to_z = jnp.where((r // 2) % 2 == 0, hub_z, end_z)
            to = at(to_z, jnp.where(r // 4 == 0, x, ox), r % 2)
            mine = jnp.logical_and(to == e, to_y == y)

            @pl.when(mine)
            def _():
                pltpu.make_async_copy(
                    tiles.at[j, r], landed.at[y, x, c, group], tile_recv.at[y, x, c, group]
                ).start()

            @pl.when(jnp.logical_not(mine))
            def _():
                tile_copy(j, r, to, to_y, group).start()

            return carry

        lax.fori_loop(first, last, one, 0)

    def drain(j):
        to_y, group = place(j)

        def one(r, carry):
            mine = jnp.logical_and(r == c, to_y == y)

            @pl.when(jnp.logical_not(mine))
            def _():
                tile_copy(j, r, e, oy, group).wait_send()

            return carry

        lax.fori_loop(0, 8, one, 0)

    @pl.when(is_hub)
    def _():
        to_x = at(hub_z, ox, c)
        to_core = at(hub_z, x, oc)
        hub_to_x = remote(f_ref, rows.at[4 + c], 3, to_x, y)
        hub_to_core = remote(f_ref, rows.at[c], 4, to_core, y)
        end_to_core = remote(cols.at[0], rows.at[2 + c], 5, to_core, y)
        other_hub_to_core = remote(rows.at[4 + c], rows.at[4 + c], 6, to_core, y)
        end_to_x = remote_pieces(cols.at[0], rows.at[6 + c], 12, to_x, y)
        other_end_to_core = remote_pieces(rows.at[6 + c], rows.at[6 + c], 16, to_core, y)
        from_core = [
            remote(rows.at[2 * i + oc], rows.at[2 * i + oc], 4 + i, to_core, y)
            for i in range(3)
        ]
        last_from_core = remote_pieces(rows.at[6 + oc], rows.at[6 + oc], 16, to_core, y)
        far_hub.start()
        hub_to_x.start()
        hub_to_core.start()
        keep = [
            pltpu.make_async_copy(f_ref, rows.at[c], local.at[1]),
            pltpu.make_async_copy(cols.at[0], rows.at[2 + c], local.at[2]),
        ]
        keep[0].start()
        send_squares()
        column_squares(1)
        near_end.wait_recv()
        for copy in end_to_x:
            copy.start()
        end_to_core.start()
        keep[1].start()
        hub_to_x.wait_recv()
        other_hub_to_core.start()
        column_squares(0)
        for copy in keep:
            copy.wait()
        for copy in from_core:
            copy.wait_recv()
        multiply(1, 0, 6, 0, depth, True)
        deliver(1, 0, 6)
        multiply(0, 0, 6, 0, depth, True)
        deliver(0, 0, 6)
        far_hub.wait_recv()
        column_squares(2)
        multiply(2, 0, 6, 0, depth, True)
        deliver(2, 0, 6)
        for k in range(PIECES):
            end_to_x[k].wait_recv()
            other_end_to_core[k].start()
            far_end[k].wait_recv()
            multiply(3, 0, 6, k * width, width, k == 0)
            if k == PIECES - 1:
                column_squares(3)
                deliver(3, 0, 6)
            last_from_core[k].wait_recv()
            for j in range(4):
                multiply(j, 6, 8, k * width, width, k == 0)
        for j in range(4):
            deliver(j, 6, 8)
        for copy in [far_hub, hub_to_x, hub_to_core, end_to_core, other_hub_to_core]:
            copy.wait_send()
        for copy in end_to_x + other_end_to_core:
            copy.wait_send()

    swap_squares.wait()
    row_scale = lax.rsqrt(squares[0][:, 0:1] + squares[1][:, 0:1] + EPS)
    for x_ in range(2):
        for c_ in range(2):
            for g_ in range(2):
                for y_ in range(2):
                    pltpu.make_async_copy(
                        landed.at[y_, x_, c_, g_],
                        landed.at[y_, x_, c_, g_],
                        tile_recv.at[y_, x_, c_, g_],
                    ).wait()
                total = landed[0, x_, c_, g_] + landed[1, x_, c_, g_]
                column_scale = lax.rsqrt(total[kept : kept + 1, 0:n] + EPS)
                o_ref[4 * g_ + 2 * x_ + c_] = (
                    unfold(total[0:kept], pad) * row_scale * column_scale
                )

    @pl.when(is_hub)
    def _():
        for j in range(4):
            drain(j)


def hub_shards(features):
    n, depth = features.shape
    kept = n - n * (128 - n) // 128
    pieces = pl.pallas_call(
        hub_kernel,
        out_shape=jax.ShapeDtypeStruct((8, n, n), jnp.float32),
        in_specs=[pl.BlockSpec(memory_space=pl.ANY)],
        out_specs=pl.BlockSpec(memory_space=pltpu.VMEM),
        scratch_shapes=[
            pltpu.VMEM((4, n, depth), jnp.bfloat16),
            pltpu.VMEM((8, n, depth), jnp.bfloat16),
            pltpu.VMEM((4, 8, n, n), jnp.float32),
            pltpu.VMEM((4, 8, kept + STAT_ROWS, 128), jnp.float32),
            pltpu.VMEM((2, 2, 2, 2, kept + STAT_ROWS, 128), jnp.float32),
            pltpu.VMEM((2, n, 128), jnp.float32),
            pltpu.SemaphoreType.DMA((20,)),
            pltpu.SemaphoreType.DMA((20,)),
            pltpu.SemaphoreType.DMA((4, 8)),
            pltpu.SemaphoreType.DMA((2, 2, 2, 2)),
            pltpu.SemaphoreType.DMA((3,)),
        ],
        compiler_params=pltpu.CompilerParams(
            collective_id=0, has_side_effects=True, vmem_limit_bytes=50 * 1024 * 1024
        ),
        name="hub_gram",
    )(features)
    return jnp.transpose(pieces, (1, 0, 2)).reshape(n, 8 * n)


def gathered_shards(features):
    local_squares = jnp.sum(jnp.square(features.astype(jnp.float32)), axis=1)
    row_norms = lax.psum(local_squares, "feat")
    every_norm = lax.all_gather(row_norms, "ex", axis=0, tiled=True)
    partial_gram = inner_tile(features, lax.all_gather(features, "ex", axis=0, tiled=True))
    gram = lax.psum_scatter(partial_gram, "feat", scatter_dimension=1, tiled=True)
    col_width = gram.shape[1]
    col_norms = lax.dynamic_slice_in_dim(
        every_norm, lax.axis_index("feat") * col_width, col_width, 0
    )
    row_scale = lax.rsqrt(row_norms + EPS)
    col_scale = lax.rsqrt(col_norms + EPS)
    return gram * row_scale[:, None] * col_scale[None, :]


def solution(mesh):
    four_groups = mesh.shape["ex"] == 16 and mesh.shape["feat"] == 2
    shards = hub_shards if four_groups else gathered_shards
    return jax.shard_map(
        shards,
        mesh=mesh,
        in_specs=(P("ex", "feat"),),
        out_specs=P("ex", "feat"),
        check_vma=False,
    )
```

time: 65.2 us -> 57 us (0.87)
  the two profiles are of different devices: /device:TPU:0 before, /device:TPU:5 now
where the time goes in v2:
time: 57 us; the launch traced here: 56.9 us
  Pallas kernels  54.6 us (96%)
  local copies, waits for them, and re-layouts  2.24 us (4%)
    pallas_call x1, Pallas kernels, hub_shards(): pl.pallas_call(hub_kernel, out_shape=jax.ShapeDtypeStruct((8, n, n), jnp....  54.6 us

profile of v2, /device:TPU:5, one launch (start us, length us, event | category | flops | bytes accessed | tf_op | source)
XLA Modules:
  0.0 56.9 jit_solution(8680827046848421464)
XLA Ops:
  0.0 0.0 copy-start
  0.0 1.1 %copy-done = bf16[96,4096]{1,0:T(8,128)(2,1)S(1)} copy-done((bf16[96,4096]{1,0:T(8,128)(2,1)S(1)}, bf16[96,4096]{1,0:T(8,128)(2,1)}, u32[]{:S(2)}) %copy-start) | copy-done | bytes 786456
  1.1 54.6 %hub_gram.1 = f32[8,96,96]{2,1,0:T(8,128)S(1)} custom-call(bf16[96,4096]{1,0:T(8,128)(2,1)S(1)} %copy-done), custom_call_target="tpu_custom_call" | custom-call | tf_op jit(solution)/shard_map/hub_gram/pallas_call | solution.py:297
  55.8 0.2 copy.2
  56.0 0.9 %reshape.3 = f32[96,768]{1,0:T(8,128)} reshape(f32[96,8,96]{2,1,0:T(8,128)S(1)} %copy.2) | data formatting | bytes 589824 | tf_op jit(solution)/shard_map/reshape | solution.py:320
Async XLA Ops:
  0.0 1.1 %copy-start = (bf16[96,4096]{1,0:T(8,128)(2,1)S(1)}, bf16[96,4096]{1,0:T(8,128)(2,1)}, u32[]{:S(2)}) copy-start(bf16[96,4096]{1,0:T(8,128)(2,1)} %f_ref.1) | copy-start | bytes 2359300

commit v3 on v2

--- a/solution.py
+++ b/solution.py
@@ -146,12 +146,21 @@
             else:
                 acc[j, first:last] += product
 
+    def across(block):
+        total = jnp.sum(jnp.transpose(lane_squares(block)), axis=0, keepdims=True)
+        return jnp.broadcast_to(total, (STAT_ROWS, n))
+
     def column_squares(j):
-        lanes = lane_squares(cols[j])
-        total = jnp.sum(jnp.transpose(lanes), axis=0, keepdims=True)
-        tiles[j, :, kept : kept + STAT_ROWS, 0:n] = jnp.broadcast_to(
-            total[None], (8, STAT_ROWS, n)
+        total = across(cols[j])
+        count = 4 if j < 2 else 8
+        tiles[j, 0:count, kept : kept + STAT_ROWS, 0:n] = jnp.broadcast_to(
+            total[None], (count, STAT_ROWS, n)
         )
+
+    def row_squares(r):
+        total = across(rows[r])
+        tiles[0, r, kept : kept + STAT_ROWS, 0:n] = total
+        tiles[1, r, kept : kept + STAT_ROWS, 0:n] = total
 
     def tile_copy(j, r, to, to_y, group):
         return pltpu.make_async_remote_copy(
@@ -191,6 +200,46 @@
 
         lax.fori_loop(first, last, one, 0)
 
+    def turned_copy(j, r, to, to_y):
+        from_c = r % 2
+        group = oh if r < 6 else h
+        return pltpu.make_async_remote_copy(
+            src_ref=tiles.at[j, r],
+            dst_ref=landed.at[y, ox, from_c, group],
+            send_sem=tile_send.at[j, r],
+            recv_sem=tile_recv.at[y, ox, from_c, group],
+            device_id=(to, to_y),
+            device_id_type=MESH,
+        )
+
+    def deliver_turned(j, r):
+        tiles[j, r, 0:kept, :] = fold(jnp.transpose(acc[j, r]), pad)
+        if j == 0:
+            turned_copy(j, r, at(end_z, x, c), h).start()
+            return
+        from_c = r % 2
+        group = oh if r < 6 else h
+
+        @pl.when(h == y)
+        def _():
+            pltpu.make_async_copy(
+                tiles.at[j, r],
+                landed.at[y, ox, from_c, group],
+                tile_recv.at[y, ox, from_c, group],
+            ).start()
+
+        @pl.when(h != y)
+        def _():
+            turned_copy(j, r, e, h).start()
+
+    def drain_turned():
+        for r in range(4, 8):
+            turned_copy(0, r, e, oy).wait_send()
+
+            @pl.when(h != y)
+            def _():
+                turned_copy(1, r, e, oy).wait_send()
+
     def drain(j):
         to_y, group = place(j)
 
@@ -203,7 +252,7 @@
 
             return carry
 
-        lax.fori_loop(0, 8, one, 0)
+        lax.fori_loop(0, 4 if j < 2 else 8, one, 0)
 
     @pl.when(is_hub)
     def _():
@@ -243,9 +292,13 @@
         for copy in from_core:
             copy.wait_recv()
         multiply(1, 0, 6, 0, depth, True)
-        deliver(1, 0, 6)
+        deliver(1, 0, 4)
         multiply(0, 0, 6, 0, depth, True)
-        deliver(0, 0, 6)
+        deliver(0, 0, 4)
+        for r in (4, 5):
+            row_squares(r)
+            deliver_turned(0, r)
+            deliver_turned(1, r)
         far_hub.wait_recv()
         column_squares(2)
         multiply(2, 0, 6, 0, depth, True)
@@ -261,8 +314,12 @@
             last_from_core[k].wait_recv()
             for j in range(4):
                 multiply(j, 6, 8, k * width, width, k == 0)
-        for j in range(4):
-            deliver(j, 6, 8)
+        deliver(3, 6, 8)
+        deliver(2, 6, 8)
+        for r in (6, 7):
+            row_squares(r)
+            deliver_turned(0, r)
+            deliver_turned(1, r)
         for copy in [far_hub, hub_to_x, hub_to_core, end_to_core, other_hub_to_core]:
             copy.wait_send()
         for copy in end_to_x + other_end_to_core:
@@ -289,6 +346,7 @@
     def _():
         for j in range(4):
             drain(j)
+        drain_turned()
 
 
 def hub_shards(features):
@@ -313,7 +371,7 @@
             pltpu.SemaphoreType.DMA((3,)),
         ],
         compiler_params=pltpu.CompilerParams(
-            collective_id=0, has_side_effects=True, vmem_limit_bytes=50 * 1024 * 1024
+            collective_id=0, has_side_effects=True, vmem_limit_bytes=62 * 1024 * 1024
         ),
         name="hub_gram",
     )(features)

time: 57 us -> 59.4 us (1.042)
  the two profiles are of different devices: /device:TPU:5 before, /device:TPU:31 now
where the time goes in v3:
time: 59.4 us; the launch traced here: 59.3 us
  Pallas kernels  57.2 us (96%)
  local copies, waits for them, and re-layouts  2.1 us (4%)
    pallas_call x1, Pallas kernels, hub_shards(): pl.pallas_call(hub_kernel, out_shape=jax.ShapeDtypeStruct((8, n, n), jnp....  57.2 us
    transpose x1, local copies, waits for them, and re-layouts, hub_shards(): return jnp.transpose(pieces, (1, 0, 2)).reshape(n, 8 * n)  1.23 us

profile of v3, /device:TPU:31, one launch (start us, length us, event | category | flops | bytes accessed | tf_op | source)
XLA Modules:
  0.0 59.3 jit_solution(3257778391209575914)
XLA Ops:
  0.0 57.2 %hub_gram.1 = f32[8,96,96]{2,1,0:T(8,128)} custom-call(bf16[96,4096]{1,0:T(8,128)(2,1)} %f_ref.1), custom_call_target="tpu_custom_call" | custom-call | tf_op jit(solution)/shard_map/hub_gram/pallas_call | solution.py:355
  57.2 1.2 %copy.2 = f32[96,8,96]{2,1,0:T(8,128)S(1)} copy(f32[96,8,96]{2,0,1:T(8,128)} %bitcast.1) | data formatting | bytes 589824 | tf_op jit(solution)/shard_map/transpose | solution.py:378
  58.4 0.9 %reshape.3 = f32[96,768]{1,0:T(8,128)} reshape(f32[96,8,96]{2,1,0:T(8,128)S(1)} %copy.2) | data formatting | bytes 589824 | tf_op jit(solution)/shard_map/reshape | solution.py:378
